TPU v7x, 32 devices: a whole 2x2x4 slice. The times are simulated.
32 devices in a mesh: row: 16 (over z, y, core), col: 2 (over x).
Axes of the slice: x: 2, y: 2, z: 4, core: 2. Of those that a mesh axis runs over, the one named last changes fastest.
Arguments:
- alignment: bfloat16 [64, 512, 64], P(None, ('col', 'row')), may hold values from -6 to 6
- pair_rep: bfloat16 [512, 512, 128], P('row', 'col'), may hold values from -128 to 128
- outer_left: bfloat16 [64, 32], replicated, may hold values from -0.75 to 0.75
- outer_right: bfloat16 [64, 32], replicated, may hold values from -0.75 to 0.75
- outer_proj: bfloat16 [1024, 128], replicated, may hold values from -1.5 to 1.5
- outer_bias: float32 [128], replicated, may hold values from -3 to 3
- average_value: bfloat16 [64, 256], replicated, may hold values from -0.75 to 0.75
- average_gate: bfloat16 [64, 256], replicated, may hold values from -0.75 to 0.75
- average_logit: bfloat16 [128, 8], replicated, may hold values from -28 to 28
- average_out: bfloat16 [256, 64], replicated, may hold values from -1 to 1
- triangle_proj: bfloat16 [128, 512], replicated, may hold values from -0.5 to 0.5
- triangle_bias: bfloat16 [128, 4], replicated, may hold values from -0.5 to 0.5
Outputs:
- pair_new: bfloat16 [512, 512, 128], P('row', 'col')
- alignment_update: bfloat16 [64, 512, 64], P(None, ('row', 'col'))
- triangle_inputs: bfloat16 [512, 512, 512], P(('col', 'row'))
- edge_bias: bfloat16 [4, 512, 512], P(None, ('col', 'row'))
All inputs are finite; a program needn't handle non-finite values.
Results may differ from a plain program's by a relative error of at most 0.02.
The roundings to bfloat16 on the way count: a program that leaves them out, or rounds other values in their place, can miss the bound.
Values may be sent and summed in bfloat16 or wider, within the bound.
A program may use at most 64 MiB of HBM per device.

v0:
```python
import jax
import jax.numpy as jnp
from jax import lax
from jax.sharding import PartitionSpec as P


def broadcast(shard, axis, root):
    mine = lax.axis_index(axis) == root
    return lax.psum(jnp.where(mine, shard, jnp.zeros_like(shard)), axis)


def standardize(values):
    widened = values.astype(jnp.float32)
    centered = widened - jnp.mean(widened, axis=-1, keepdims=True)
    spread = jnp.mean(centered * centered, axis=-1, keepdims=True)
    return centered * lax.rsqrt(spread + 1e-05)


def per_device(
    alignment,
    pair_rep,
    outer_left,
    outer_right,
    outer_proj,
    outer_bias,
    average_value,
    average_gate,
    average_logit,
    average_out,
    triangle_proj,
    triangle_bias,
):
    row_devices = lax.axis_size("row")
    col_devices = lax.axis_size("col")
    local_row_index = lax.axis_index("row")
    col_index = lax.axis_index("col")
    sequence_count, slab_length, alignment_channel_width = alignment.shape
    row_window, cols_tile, pair_width = pair_rep.shape
    factor_width = outer_left.shape[1]
    head_count = average_logit.shape[1]
    value_width = average_value.shape[1]
    head_width = value_width // head_count
    alignment_layer_norm = standardize(alignment).astype(jnp.bfloat16)
    normalized_flat_rows = alignment_layer_norm.reshape(
        sequence_count, slab_length * alignment_channel_width
    )
    normalized_columns = lax.all_gather(normalized_flat_rows, "row", axis=1, tiled=True)
    norm_wide = normalized_columns.reshape(sequence_count, cols_tile, alignment_channel_width)
    right_cols = jnp.dot(norm_wide, outer_right, preferred_element_type=jnp.float32).astype(
        jnp.bfloat16
    )
    value_cols = jnp.dot(norm_wide, average_value, preferred_element_type=jnp.float32).astype(
        jnp.bfloat16
    )
    group_member_count = row_devices // col_devices
    start_position = local_row_index % group_member_count * (row_window * alignment_channel_width)
    local_rows = lax.dynamic_slice_in_dim(
        normalized_columns, start_position, row_window * alignment_channel_width, 1
    )
    norm_rows = broadcast(local_rows, "col", local_row_index // group_member_count).reshape(
        sequence_count, row_window, alignment_channel_width
    )
    left_rows = jnp.dot(norm_rows, outer_left, preferred_element_type=jnp.float32).astype(
        jnp.bfloat16
    )
    row_block = 8
    block_count = row_window // row_block
    left_blocks = jnp.transpose(
        left_rows.reshape(sequence_count, block_count, row_block * factor_width), (1, 0, 2)
    )
    right_flat = right_cols.reshape(sequence_count, cols_tile * factor_width)

    def pair_block(block_items):
        left_flat, pair_rows = block_items
        outer_sum = lax.dot_general(
            left_flat, right_flat, (((0,), (0,)), ((), ())), preferred_element_type=jnp.float32
        )
        outer_sum = jnp.transpose(
            outer_sum.reshape(row_block, factor_width, cols_tile, factor_width), (0, 2, 1, 3)
        )
        outer_mean = (
            outer_sum.reshape(row_block, cols_tile, factor_width * factor_width) / sequence_count
        ).astype(jnp.bfloat16)
        update = jnp.dot(outer_mean, outer_proj, preferred_element_type=jnp.float32)
        return (pair_rows.astype(jnp.float32) + update + outer_bias).astype(jnp.bfloat16)

    pair_new = lax.map(
        pair_block, (left_blocks, pair_rep.reshape(block_count, row_block, cols_tile, pair_width))
    )
    pair_new = pair_new.reshape(row_window, cols_tile, pair_width)
    pair_norm = standardize(pair_new).astype(jnp.bfloat16)
    logits = jnp.einsum("ijc,ch->hij", pair_norm, average_logit, preferred_element_type=jnp.float32)
    peak_values = lax.pmax(jnp.max(logits, axis=2), "col")
    weights = jnp.exp(logits - peak_values[:, :, None]).astype(jnp.bfloat16)
    denom_part = jnp.sum(weights.astype(jnp.float32), axis=2)
    value_heads = value_cols.reshape(sequence_count, cols_tile, head_count, head_width)
    numer_part = jnp.einsum(
        "hij,sjhc->ishc", weights, value_heads, preferred_element_type=jnp.float32
    )
    numer_part = numer_part.reshape(row_window, sequence_count, value_width)
    out_wide = average_out.astype(jnp.float32)
    numer_sub, denom_sub = (
        lax.psum_scatter(
            numer_part.astype(jnp.bfloat16), "col", scatter_dimension=0, tiled=True
        ).astype(jnp.float32),
        lax.psum_scatter(
            denom_part.astype(jnp.bfloat16), "col", scatter_dimension=1, tiled=True
        ).astype(jnp.float32),
    )
    sub_len = numer_sub.shape[0]
    norm_sub = lax.dynamic_slice_in_dim(norm_rows, col_index * sub_len, sub_len, 1)
    gate_vals = jax.nn.sigmoid(jnp.dot(norm_sub, average_gate, preferred_element_type=jnp.float32))
    gate_vals = gate_vals.reshape(sequence_count, sub_len, head_count, head_width)
    numer_moved = jnp.transpose(
        numer_sub.reshape(sub_len, sequence_count, head_count, head_width), (1, 0, 2, 3)
    )
    gated_vals = (gate_vals * numer_moved / jnp.transpose(denom_sub)[None, :, :, None]).reshape(
        sequence_count, sub_len, value_width
    )
    alignment_update = jnp.dot(gated_vals, out_wide, precision=lax.Precision.HIGHEST).astype(
        jnp.bfloat16
    )
    piece_len = cols_tile // row_devices
    shaped = pair_norm.reshape(row_window, row_devices, piece_len, pair_width)
    split_at = 3 * (triangle_proj.shape[1] // 4)
    turned = lax.all_to_all(shaped, "row", split_axis=1, concat_axis=0, tiled=True)[:, 0]
    projected = jnp.einsum("jic,cd->ijd", turned, triangle_proj, preferred_element_type=jnp.float32)
    inputs = jnp.concatenate(
        [projected[..., :split_at], jax.nn.sigmoid(projected[..., split_at:])], axis=-1
    ).astype(jnp.bfloat16)
    bias_rows = jnp.einsum(
        "jic,ch->ihj", turned, triangle_bias, preferred_element_type=jnp.float32
    ).astype(jnp.bfloat16)
    triangle_inputs, bias_rows = (inputs, bias_rows)
    edge_bias = jnp.transpose(bias_rows, (1, 0, 2))
    return (pair_new, alignment_update, triangle_inputs, edge_bias)


def solution(mesh):
    placed = (
        P(None, ("col", "row"), None),
        P("row", "col", None),
        P(),
        P(),
        P(),
        P(),
        P(),
        P(),
        P(),
        P(),
        P(),
        P(),
    )
    return jax.shard_map(
        per_device,
        mesh=mesh,
        in_specs=placed,
        out_specs=(
            P("row", "col", None),
            P(None, ("row", "col"), None),
            P(("col", "row"), None, None),
            P(None, ("col", "row"), None),
        ),
        check_vma=False,
    )
```

profile of v0, /device:TPU:0, one launch (start us, length us, event | category | flops | bytes accessed | tf_op | source)
XLA Modules:
  0.0 261.1 jit_solution(14261829900147095496)
XLA Ops:
  12.1 44.2 %all-gather.2.cloned.1.call-done = bf16[64,16384]{1,0:T(8,128)(2,1)} async-done(((bf16[64,1024]{1,0:T(8,128)(2,1)}), bf16[64,16384]{1,0:T(8,128)(2,1)}) %all-gather.2.cloned.1.call-update) | async-done | bytes 2097168 | tf_op jit(solution)/shard_map/all_gather | solution.py:47
  59.0 5.5 %reshape.119 = bf16[64,256,64]{2,1,0:T(8,128)(2,1)} reshape(bf16[64,16384]{1,0:T(8,128)(2,1)S(1)} %copy-done.4) | data formatting | bytes 4194304 | tf_op jit(solution)/shard_map/reshape | solution.py:48
  64.5 8.1 %convolution_convert_fusion = bf16[64,256,256]{1,2,0:T(8,128)(2,1)} fusion(bf16[64,256,64]{2,1,0:T(8,128)(2,1)} %reshape.119, bf16[64,256]{1,0:T(8,128)(2,1)S(1)} %copy-done.8), kind=kOutput, calls=%fused_computation.15 | convolution fusion | flops 541065216 | bytes 10518528 | tf_op jit(solution)/shard_map/dot_general | solution.py:52
  74.2 3.6 %copy.50 = bf16[64,256,32]{0,2,1:T(8,128)(2,1)S(1)} copy(bf16[64,256,32]{1,2,0:T(8,128)(2,1)S(1)} %convolution_convert_fusion.1) | data formatting | bytes 2097152 | tf_op jit(solution)/shard_map/convert_element_type | solution.py:49
  77.7 8.8 %all-reduce.2.cloned.1.call-done = bf16[64,32,64]{2,0,1:T(8,128)(2,1)} async-done(((bf16[64,32,64]{2,0,1:T(8,128)(2,1)}), bf16[64,32,64]{2,0,1:T(8,128)(2,1)}) %all-reduce.2.cloned.1.call-update) | async-done | bytes 262160 | tf_op jit(solution)/shard_map/psum | solution.py:9
  88.1 37.9 %while.10 = (s32[]{:T(128)}, bf16[4,8,256,128]{3,2,1,0:T(8,128)(2,1)}, bf16[4,8,256,128]{3,2,1,0:T(8,128)(2,1)}, bf16[4,64,256]{1,2,0:T(8,128)(2,1)S(1)}, bf16[6...) while((s32[]{:T(128)}, bf16[4,8,256,128]{3,2,1,0:T(8,128)(2,1)}, ...), condition=%wide.region_4.5_spmd, body=%wide.region_3.4_spmd.sunk | while | flops 810549248 | bytes 23429816 | solution.py:87
  94.4 3.2 %fusion.63 = bf16[4,8,256,128]{3,2,1,0:T(8,128)(2,1)} fusion(bf16[4,8,256,128]{3,2,1,0:T(8,128)(2,1)} %get-tuple-element.126, s32[]{:T(128)S(6)} %copy.92, bf16[8,256,1024]{1,2,0:T(8,128)(2,1)S(1)} %bitcast.121, f32[128]{0:T(128)S(1)} %get-tuple-element.139, bf16[4,8,256,128]{3,2,1,0:T(8,128)(2,1)} %get-tuple-element.135, ...), kind=kOutput, calls=%fused_computation.6.clone.1 | convolution fusion | flops 537919488 | bytes 5505540 | tf_op jit(solution)/shard_map/while/body/eval_jaxpr/dot_general | solution.py:84
  103.9 3.2 %fusion.63 = bf16[4,8,256,128]{3,2,1,0:T(8,128)(2,1)} fusion(bf16[4,8,256,128]{3,2,1,0:T(8,128)(2,1)} %get-tuple-element.126, s32[]{:T(128)S(6)} %copy.92, bf16[8,256,1024]{1,2,0:T(8,128)(2,1)S(1)} %bitcast.121, f32[128]{0:T(128)S(1)} %get-tuple-element.139, bf16[4,8,256,128]{3,2,1,0:T(8,128)(2,1)} %get-tuple-element.135, ...), kind=kOutput, calls=%fused_computation.6.clone.1 | convolution fusion | flops 537919488 | bytes 5505540 | tf_op jit(solution)/shard_map/while/body/eval_jaxpr/dot_general | solution.py:84
  113.3 3.2 %fusion.63 = bf16[4,8,256,128]{3,2,1,0:T(8,128)(2,1)} fusion(bf16[4,8,256,128]{3,2,1,0:T(8,128)(2,1)} %get-tuple-element.126, s32[]{:T(128)S(6)} %copy.92, bf16[8,256,1024]{1,2,0:T(8,128)(2,1)S(1)} %bitcast.121, f32[128]{0:T(128)S(1)} %get-tuple-element.139, bf16[4,8,256,128]{3,2,1,0:T(8,128)(2,1)} %get-tuple-element.135, ...), kind=kOutput, calls=%fused_computation.6.clone.1 | convolution fusion | flops 537919488 | bytes 5505540 | tf_op jit(solution)/shard_map/while/body/eval_jaxpr/dot_general | solution.py:84
  120.2 2.6 copy.87
  122.8 3.2 %fusion.63 = bf16[4,8,256,128]{3,2,1,0:T(8,128)(2,1)} fusion(bf16[4,8,256,128]{3,2,1,0:T(8,128)(2,1)} %get-tuple-element.126, s32[]{:T(128)S(6)} %copy.92, bf16[8,256,1024]{1,2,0:T(8,128)(2,1)S(1)} %bitcast.121, f32[128]{0:T(128)S(1)} %get-tuple-element.139, bf16[4,8,256,128]{3,2,1,0:T(8,128)(2,1)} %get-tuple-element.135, ...), kind=kOutput, calls=%fused_computation.6.clone.1 | convolution fusion | flops 537919488 | bytes 5505540 | tf_op jit(solution)/shard_map/while/body/eval_jaxpr/dot_general | solution.py:84
  128.4 3.6 %multiply_reduce_fusion = f32[4,8,256]{2,1,0:T(8,128)S(1)} fusion(f32[4,8,256]{2,1,0:T(8,128)S(1)} %get-tuple-element.71, bf16[4,8,256,128]{3,2,1,0:T(8,128)(2,1)} %get-tuple-element.41), kind=kLoop, calls=%fused_computation.23 | loop fusion | flops 4186112 | bytes 2162688 | tf_op jit(solution)/shard_map/reduce_sum | solution.py:15
  132.1 3.2 %copy.58 = f32[4,8,256,128]{3,1,0,2:T(8,128)} copy(bf16[4,8,256,128]{3,2,1,0:T(8,128)(2,1)S(1)} %copy-done.3) | data formatting | bytes 6291456 | tf_op jit(solution)/shard_map/convert_element_type | solution.py:13
  135.7 5.3 %multiply_convert_fusion.1 = bf16[32,16,16,128]{3,0,2,1:T(8,128)(2,1)} fusion(f32[32,16,16,128]{3,0,2,1:T(8,128)} %bitcast.128, f32[32,16,16]{0,2,1:T(8,128)S(1)} %copy.60, f32[32,16,16]{0,2,1:T(8,128)S(1)} %copy.59), kind=kLoop, calls=%fused_computation.20 | loop fusion | flops 3145728 | bytes 6356992 | tf_op jit(solution)/shard_map/convert_element_type | solution.py:91
  141.1 5.7 %all-to-all-start = ((bf16[32,16,16,128]{3,0,2,1:T(8,128)(2,1)}), bf16[32,16,16,128]{3,0,2,1:T(8,128)(2,1)}, u32[]{:S(2)}, u32[]{:S(2)}) async-start(bf16[32,16,16,128]{3,0,2,1:T(8,128)(2,1)} %multiply_convert_fusion.1), calls=%async_computation.2 | async-start | bytes 4194304 | tf_op jit(solution)/shard_map/all_to_all | solution.py:126
  146.8 6.4 %fusion.43 = (f32[8,32]{0,1:T(8,128)S(1)}, f32[8,32,256]{2,0,1:T(8,128)S(1)}) fusion(bf16[128,8]{0,1:T(8,128)(2,1)S(1)} %copy-done.15, bf16[32,256,128]{2,1,0:T(8,128)(2,1)S(1)} %bitcast.125, f32[32,256]{1,0:T(8,128)S(1)} %get-tuple-element.69, f32[32,256]{1,0:T(8,128)S(1)} %get-tuple-element.70), kind=kOutput, calls=%fused_computation.70 | convolution fusion | flops 21036800 | bytes 2427904 | tf_op jit(solution)/shard_map/ijc,ch->hij/dot_general | solution.py:92
  153.2 7.2 %pmax.7 = f32[8,32]{0,1:T(8,128)S(1)} all-reduce(f32[8,32]{0,1:T(8,128)S(1)} %get-tuple-element.72), channel_id=1, replica_groups=mesh['row'=16,'col'=2] {'col'}, use_global_device_ids=true, to_apply=%region_8.9 | all-reduce | flops 256 | bytes 2048 | tf_op jit(solution)/shard_map/pmax | solution.py:93
  161.4 7.6 %convert_bitcast_fusion = bf16[32,64,8,32]{0,3,1,2:T(8,128)(2,1)} fusion(bf16[64,256,8,32]{1,3,2,0:T(8,128)(2,1)} %bitcast.132, bf16[8,32,256,1]{2,0,1,3:T(8,128)(2,1)S(1)} %fusion.36), kind=kOutput, calls=%fused_computation.21 | convolution fusion | flops 268959744 | bytes 9568256 | tf_op jit(solution)/shard_map/hij,sjhc->ishc/dot_general | solution.py:97
  169.1 8.2 %copy.56 = bf16[32,64,8,32]{1,3,2,0:T(8,128)(2,1)} copy(bf16[32,64,8,32]{0,3,1,2:T(8,128)(2,1)} %convert_bitcast_fusion) | data formatting | bytes 2097152 | tf_op jit(solution)/shard_map/convert_element_type | solution.py:104
  179.2 31.3 %reduce-scatter.3.cloned.1.call-done = bf16[16,64,256]{1,2,0:T(8,128)(2,1)} async-done(((bf16[32,64,256]{1,2,0:T(8,128)(2,1)}), bf16[16,64,256]{1,2,0:T(8,128)(2,1)}) %reduce-scatter.3.cloned.1.call-update) | async-done | bytes 524304 | tf_op jit(solution)/shard_map/reduce_scatter | solution.py:103
  219.2 5.7 %copy-done.1 = f32[16,512,512]{1,2,0:T(8,128)} copy-done((f32[16,512,512]{1,2,0:T(8,128)}, f32[16,512,512]{1,2,0:T(8,128)S(1)}, u32[]{:S(2)}) %copy-start.1) | copy-done | bytes 16777240
  226.1 8.2 %slice.21 = bf16[16,512,384]{1,2,0:T(8,128)(2,1)} slice(f32[16,512,512]{1,2,0:T(8,128)} %copy-done.1), slice={[0:16], [0:512], [0:384]} | slice | bytes 12582912 | tf_op jit(solution)/shard_map/slice | solution.py:129
  235.5 6.8 %pad_maximum_fusion = bf16[16,512,512]{1,2,0:T(8,128)(2,1)} fusion(bf16[16,512,128]{1,2,0:T(8,128)(2,1)S(1)} %fusion.12, bf16[16,512,384]{1,2,0:T(8,128)(2,1)} %slice.21), kind=kLoop, calls=%fused_computation.12 | loop fusion | flops 16777216 | bytes 16777216 | tf_op jit(solution)/shard_map/concatenate | solution.py:128
  242.3 12.3 %copy.64 = bf16[16,512,512]{2,1,0:T(8,128)(2,1)} copy(bf16[16,512,512]{1,2,0:T(8,128)(2,1)} %pad_maximum_fusion) | data formatting | bytes 16777216
  (109 shorter events, 49.9 us)
Async XLA Ops:
  7.2 209.7 %copy-start = (bf16[128,512]{1,0:T(8,128)(2,1)S(1)}, bf16[128,512]{1,0:T(8,128)(2,1)}, u32[]{:S(2)}) copy-start(bf16[128,512]{1,0:T(8,128)(2,1)} %param.24) | copy-start | bytes 393220
  7.2 49.0 %all-gather.2.cloned.1.call-start = ((), (), s32[]{:S(2)}) async-start(), calls=%async_computation.3 | async-start | bytes 2228224 | tf_op jit(solution)/shard_map/all_gather | solution.py:47
  11.9 74.5 %all-reduce.2.cloned.1.call-start = ((), (), s32[]{:S(2)}) async-start(), calls=%async_computation.4 | async-start | bytes 1048576 | tf_op jit(solution)/shard_map/psum | solution.py:9
  56.2 2.7 %copy-start.4 = (bf16[64,16384]{1,0:T(8,128)(2,1)S(1)}, bf16[64,16384]{1,0:T(8,128)(2,1)}, u32[]{:S(2)}) copy-start(bf16[64,16384]{1,0:T(8,128)(2,1)} %all-gather.2.cloned.1.call-done) | copy-start | bytes 6291460
  57.4 7.1 %copy-start.8 = (bf16[64,256]{1,0:T(8,128)(2,1)S(1)}, bf16[64,256]{1,0:T(8,128)(2,1)}, u32[]{:S(2)}) copy-start(bf16[64,256]{1,0:T(8,128)(2,1)} %param.20) | copy-start | bytes 98308
  64.5 8.1 %copy-start.2 = (bf16[64,256,64]{2,1,0:T(8,128)(2,1)S(1)}, bf16[64,256,64]{2,1,0:T(8,128)(2,1)}, u32[]{:S(2)}) copy-start(bf16[64,256,64]{2,1,0:T(8,128)(2,1)} %reshape.119) | copy-start | bytes 6291460
  64.5 8.1 %copy-start.10 = (bf16[64,32]{0,1:T(8,128)(2,1)S(1)}, bf16[64,32]{0,1:T(8,128)(2,1)}, u32[]{:S(2)}) copy-start(bf16[64,32]{0,1:T(8,128)(2,1)} %param.17) | copy-start | bytes 12292
  72.6 13.9 %copy-start.11 = (bf16[64,32]{0,1:T(8,128)(2,1)S(1)}, bf16[64,32]{0,1:T(8,128)(2,1)}, u32[]{:S(2)}) copy-start(bf16[64,32]{0,1:T(8,128)(2,1)} %param.16) | copy-start | bytes 12292
  72.6 15.5 %copy-start.16 = (f32[128]{0:T(128)S(1)}, f32[128]{0:T(128)}, u32[]{:S(2)}) copy-start(f32[128]{0:T(128)} %param.19) | copy-start | bytes 1540
  91.8 2.6 %copy-start.13 = (bf16[1024,128]{1,0:T(8,128)(2,1)S(1)}, bf16[1024,128]{1,0:T(8,128)(2,1)}, u32[]{:S(2)}) copy-start(bf16[1024,128]{1,0:T(8,128)(2,1)} %get-tuple-element.138) | copy-start | bytes 786436 | tf_op jit(solution)/shard_map/while
  94.4 3.2 %copy-start.6 = (bf16[4,64,256]{1,2,0:T(8,128)(2,1)S(1)}, bf16[4,64,256]{1,2,0:T(8,128)(2,1)}, u32[]{:S(2)}) copy-start(bf16[4,64,256]{1,2,0:T(8,128)(2,1)} %copy-done.5) | copy-start | bytes 393220 | tf_op jit(solution)/shard_map/while
  103.9 3.2 %copy-start.6 = (bf16[4,64,256]{1,2,0:T(8,128)(2,1)S(1)}, bf16[4,64,256]{1,2,0:T(8,128)(2,1)}, u32[]{:S(2)}) copy-start(bf16[4,64,256]{1,2,0:T(8,128)(2,1)} %copy-done.5) | copy-start | bytes 393220 | tf_op jit(solution)/shard_map/while
  113.3 3.2 %copy-start.6 = (bf16[4,64,256]{1,2,0:T(8,128)(2,1)S(1)}, bf16[4,64,256]{1,2,0:T(8,128)(2,1)}, u32[]{:S(2)}) copy-start(bf16[4,64,256]{1,2,0:T(8,128)(2,1)} %copy-done.5) | copy-start | bytes 393220 | tf_op jit(solution)/shard_map/while
  122.8 3.2 %copy-start.6 = (bf16[4,64,256]{1,2,0:T(8,128)(2,1)S(1)}, bf16[4,64,256]{1,2,0:T(8,128)(2,1)}, u32[]{:S(2)}) copy-start(bf16[4,64,256]{1,2,0:T(8,128)(2,1)} %copy-done.5) | copy-start | bytes 393220 | tf_op jit(solution)/shard_map/while
  126.0 6.1 %copy-start.3 = (bf16[4,8,256,128]{3,2,1,0:T(8,128)(2,1)S(1)}, bf16[4,8,256,128]{3,2,1,0:T(8,128)(2,1)}, u32[]{:S(2)}) copy-start(bf16[4,8,256,128]{3,2,1,0:T(8,128)(2,1)} %get-tuple-element.41) | copy-start | bytes 6291460
  135.7 11.1 %copy-start.15 = (bf16[128,8]{0,1:T(8,128)(2,1)S(1)}, bf16[128,8]{0,1:T(8,128)(2,1)}, u32[]{:S(2)}) copy-start(bf16[128,8]{0,1:T(8,128)(2,1)} %param.22) | copy-start | bytes 6148
  141.1 73.6 %all-to-all-start = ((bf16[32,16,16,128]{3,0,2,1:T(8,128)(2,1)}), bf16[32,16,16,128]{3,0,2,1:T(8,128)(2,1)}, u32[]{:S(2)}, u32[]{:S(2)}) async-start(bf16[32,16,16,128]{3,0,2,1:T(8,128)(2,1)} %multiply_convert_fusion.1), calls=%async_computation.2 | async-start | bytes 4194304 | tf_op jit(solution)/shard_map/all_to_all | solution.py:126
  146.8 31.7 %reduce-scatter.5.cloned.1.call-start = ((), (), s32[]{:S(2)}) async-start(), calls=%async_computation.6 | async-start | bytes 12288 | tf_op jit(solution)/shard_map/reduce_scatter | solution.py:106
  161.3 49.2 %reduce-scatter.3.cloned.1.call-start = ((), (), s32[]{:S(2)}) async-start(), calls=%async_computation.5 | async-start | bytes 3145728 | tf_op jit(solution)/shard_map/reduce_scatter | solution.py:103
  169.1 8.2 %copy-start.7 = (bf16[64,32,64]{2,0,1:T(8,128)(2,1)S(1)}, bf16[64,32,64]{2,0,1:T(8,128)(2,1)}, u32[]{:S(2)}) copy-start(bf16[64,32,64]{2,0,1:T(8,128)(2,1)} %all-reduce.2.cloned.1.call-done) | copy-start | bytes 786436
  169.1 8.2 %copy-start.14 = (bf16[64,256]{1,0:T(8,128)(2,1)S(1)}, bf16[64,256]{1,0:T(8,128)(2,1)}, u32[]{:S(2)}) copy-start(bf16[64,256]{1,0:T(8,128)(2,1)} %param.21) | copy-start | bytes 98308
  177.8 34.2 %copy-start.9 = (bf16[256,64]{0,1:T(8,128)(2,1)S(1)}, bf16[256,64]{0,1:T(8,128)(2,1)}, u32[]{:S(2)}) copy-start(bf16[256,64]{0,1:T(8,128)(2,1)} %param.23) | copy-start | bytes 98308
  219.2 5.7 %copy-start.1 = (f32[16,512,512]{1,2,0:T(8,128)}, f32[16,512,512]{1,2,0:T(8,128)S(1)}, u32[]{:S(2)}) copy-start(f32[16,512,512]{1,2,0:T(8,128)S(1)} %convolution_bitcast_fusion) | copy-start | bytes 50331652
  226.1 8.2 %copy-start.12 = (bf16[128,4]{0,1:T(4,128)(2,1)S(1)}, bf16[128,4]{0,1:T(4,128)(2,1)}, u32[]{:S(2)}) copy-start(bf16[128,4]{0,1:T(4,128)(2,1)} %param.25) | copy-start | bytes 3076
  (7 other events, 10.7 us)
Sparse Core Ops, SparseCore 0:
  12.1 44.1 all-gather.1
  59.1 27.3 all-reduce.1
  161.4 10.9 reduce-scatter.4
  177.4 33.0 reduce-scatter.2
where the time goes:
time: 262 us; the launch traced here: 261 us
  waiting for transfers between devices  84.3 us (32%)
  local copies, waits for them, and re-layouts  73.9 us (28%)
  matrix products  48.3 us (18%)
  other arithmetic  27.2 us (10%)
  between operations  14.1 us (5%)
  blocking collectives  7.22 us (3%)
  starting transfers between devices  5.83 us (2%)
    all_gather x1, waiting for transfers between devices, per_device(): lax.all_gather(normalized_flat_rows, 'row', axis=1, tiled=True)  44.2 us
    reduce_scatter x1, waiting for transfers between devices, per_device(): lax.psum_scatter(numer_part.astype(jnp.bfloat16), 'col', scatter_dimensio...  31.3 us
    unnamed x31, local copies, waits for them, and re-layouts  19.6 us
    dot_general x4, matrix products, pair_block(): update = jnp.dot(outer_mean, outer_proj, preferred_element_type=jnp.float32)  12.8 us
    convert_element_type x4, local copies, waits for them, and re-layouts, pair_block(): outer_mean = (outer_sum.reshape(row_block, cols_tile, factor_width * fact...  10.4 us
    psum x1, waiting for transfers between devices, broadcast(): return lax.psum(jnp.where(mine, shard, jnp.zeros_like(shard)), axis)  8.76 us
    convert_element_type x1, local copies, waits for them, and re-layouts, per_device(): numer_part.astype(jnp.bfloat16)  8.16 us
    slice x1, local copies, waits for them, and re-layouts, per_device(): projected[..., :split_at]  8.16 us
  transfers between devices with their start and end apart: 5, of which 3 were waited for; matrix products, arithmetic and copies ran while one was open for 18% of the time, Pallas kernels for 0%

commit v1 on v0

--- a/solution.py
+++ b/solution.py
@@ -1,7 +1,15 @@
+import functools
 import jax
 import jax.numpy as jnp
 from jax import lax
 from jax.sharding import PartitionSpec as P
+from jax.experimental import pallas as pl
+from jax.experimental.pallas import tpu as pltpu
+
+MESH = pl.DeviceIdType.MESH
+BF16 = jnp.bfloat16
+F32 = jnp.float32
+NT = (((1,), (1,)), ((), ()))
 
 
 def broadcast(shard, axis, root):
@@ -136,6 +144,469 @@
     return (pair_new, alignment_update, triangle_inputs, edge_bias)
 
 
+def dot_nt(a, b):
+    return lax.dot_general(a, b, NT, preferred_element_type=F32)
+
+
+def dot_nn(a, b):
+    return jnp.dot(a, b, preferred_element_type=F32)
+
+
+def gather_kernel(rows_n, align_ref, cols_ref, rows_ref, own, send_sem, recv_sem, row_sem):
+    half, slab = own.shape[0], own.shape[1]
+    r, c = lax.axis_index("row"), lax.axis_index("col")
+    far = rows_n // 4
+    a, b, e = r // 4, (r // 2) % 2, r % 2
+
+    def place(a_, b_, e_):
+        return (a_ * 4 + b_ * 2 + e_, c)
+
+    across = (a, 1 - b, e)
+    beside = (a, b, 1 - e)
+    distant = [(lax.rem(a + k, far), b, e) for k in range(1, far)]
+    shard = c * rows_n + r
+    owner = (shard // 2, 1 - c)
+    source_col = (2 * r) // rows_n
+    source_row = lax.rem(2 * r, rows_n)
+    barrier = pltpu.get_barrier_semaphore()
+    for spot in distant + [across, beside]:
+        pl.semaphore_signal(barrier, inc=1, device_id=place(*spot), device_id_type=MESH)
+
+    @pl.when(source_col != c)
+    def _():
+        for k in range(2):
+            pl.semaphore_signal(
+                barrier, inc=1, device_id=(source_row + k, source_col), device_id_type=MESH
+            )
+
+    wide = align_ref[...].astype(F32)
+    centered = wide - jnp.mean(wide, axis=-1, keepdims=True)
+    spread = jnp.mean(centered * centered, axis=-1, keepdims=True)
+    norm = centered * lax.rsqrt(spread + 1e-05)
+    own[...] = jnp.concatenate([norm[:half], norm[half:]], axis=-1).astype(BF16)
+    pl.semaphore_wait(barrier, far + 2)
+
+    def window(index):
+        return cols_ref.at[:, pl.ds(pl.multiple_of(index * slab, slab), slab), :]
+
+    started = []
+
+    def send(src, index, target):
+        copy = pltpu.make_async_remote_copy(
+            src_ref=src,
+            dst_ref=window(index),
+            send_sem=send_sem.at[len(started)],
+            recv_sem=recv_sem.at[index],
+            device_id=target,
+            device_id_type=MESH,
+        )
+        copy.start()
+        started.append(copy)
+
+    def arrived(index):
+        pltpu.make_async_remote_copy(
+            src_ref=own,
+            dst_ref=window(index),
+            send_sem=send_sem.at[0],
+            recv_sem=recv_sem.at[index],
+            device_id=place(*beside),
+            device_id_type=MESH,
+        ).wait_recv()
+
+    for spot in distant:
+        send(own, r, place(*spot))
+    send(own, r, place(*across))
+    send(own, r, place(*beside))
+    row_copy = pltpu.make_async_remote_copy(
+        src_ref=own,
+        dst_ref=rows_ref.at[:, pl.ds(pl.multiple_of(lax.rem(shard, 2) * slab, slab), slab), :],
+        send_sem=send_sem.at[len(started)],
+        recv_sem=row_sem.at[lax.rem(shard, 2)],
+        device_id=owner,
+        device_id_type=MESH,
+    )
+    row_copy.start()
+    started.append(row_copy)
+    window(r)[...] = own[...]
+
+    def index_of(spot):
+        return spot[0] * 4 + spot[1] * 2 + spot[2]
+
+    def forward(spot, both):
+        index = index_of(spot)
+        arrived(index)
+        if both:
+            send(window(index), index, place(*across))
+        send(window(index), index, place(*beside))
+
+    forward(across, False)
+    for k in range(far - 1, 0, -1):
+        spot = (lax.rem(a + k, far), b, e)
+        forward(spot, True)
+    for k in range(far - 1, 0, -1):
+        forward((lax.rem(a + k, far), 1 - b, e), False)
+    for k in [0] + list(range(far - 1, 0, -1)):
+        for flip in range(2):
+            arrived(index_of((lax.rem(a + k, far), b if flip == 0 else 1 - b, 1 - e)))
+
+    @pl.when(source_col == c)
+    def _():
+        rows_ref[...] = cols_ref[
+            :, pl.ds(pl.multiple_of(source_row * slab, 2 * slab), 2 * slab), :
+        ]
+
+    @pl.when(source_col != c)
+    def _():
+        for k in range(2):
+            pltpu.make_async_remote_copy(
+                src_ref=own,
+                dst_ref=rows_ref.at[:, k * slab : (k + 1) * slab, :],
+                send_sem=send_sem.at[0],
+                recv_sem=row_sem.at[k],
+                device_id=owner,
+                device_id_type=MESH,
+            ).wait_recv()
+
+    for copy in started:
+        copy.wait_send()
+
+
+def pair_kernel(
+    rows_n, heads, cols_ref, rows_ref, pair_ref, right_ref, left_ref, proj_ref, bias_ref, value_ref,
+    gate_ref, logit_ref, out_ref, new_ref, update_ref, turned_ref, rs, rb, nr, lt, outer, spun, ready,
+    lg, num, stat, nsend, nrecv, ssend, srecv, turn_send, turn_recv, local_sem, col_send, col_recv,
+):
+    half, tile, lanes = cols_ref.shape
+    rows = rows_ref.shape[1]
+    slab = tile // rows_n
+    width = right_ref.shape[0] // 2
+    block = 8
+    chunk = slab
+    span = heads * rows
+    r, c = lax.axis_index("row"), lax.axis_index("col")
+    barrier = pltpu.get_barrier_semaphore()
+
+    @pl.loop(1, rows_n)
+    def _(k):
+        pl.semaphore_signal(
+            barrier, inc=1, device_id=(lax.rem(r + k, rows_n), c), device_id_type=MESH
+        )
+
+    pl.semaphore_signal(barrier, inc=1, device_id=(r, 1 - c), device_id_type=MESH)
+
+    @pl.loop(0, half)
+    def _(s):
+        res = dot_nt(right_ref[...], cols_ref[s])
+        for t in range(tile // 128):
+            piece = res[:, t * 128 : (t + 1) * 128]
+            rs[t, pl.ds(pl.multiple_of(s * width, width), width), :] = piece[:width]
+            rs[t, pl.ds(pl.multiple_of((half + s) * width, width), width), :] = piece[width:]
+
+    for d in range(width):
+        for t in range(tile // 128):
+            at = d * tile + t * 128
+            rb[:, at : at + 128] = rs.at[t][pl.ds(d, 2 * half, stride=width), :].astype(BF16)
+
+    nr[...] = rows_ref[...].astype(F32).reshape(half * rows, lanes)
+    for i in range(rows):
+        token = nr[pl.ds(i, half, stride=rows), :].astype(BF16)
+        res = dot_nt(left_ref[...], token)
+        lt[i * width : (i + 1) * width, :] = jnp.concatenate(
+            [res[:width], res[width:]], axis=1
+        ).astype(BF16)
+
+    def do_block(base, place):
+        left = lt[pl.ds(pl.multiple_of(base * width, block * width), block * width), :]
+        for d in range(width):
+            res = dot_nn(left, rb[:, d * tile : (d + 1) * tile]).astype(BF16)
+            outer[:, d * width : (d + 1) * width, :] = res.reshape(block, width, tile)
+
+        @pl.loop(0, block)
+        def _(k):
+            i = base + k
+            update = dot_nn(proj_ref[...], outer[k]).T
+            fresh = (pair_ref[i].astype(F32) + update + bias_ref[...]).astype(BF16)
+            new_ref[i] = fresh
+            wide = fresh.astype(F32)
+            centered = wide - jnp.mean(wide, axis=-1, keepdims=True)
+            spread = jnp.mean(centered * centered, axis=-1, keepdims=True)
+            norm = (centered * lax.rsqrt(spread + 1e-05)).astype(BF16)
+            logit = dot_nt(logit_ref[...], norm)
+            for t in range(tile // 128):
+                lg.at[t][pl.ds(i, heads, stride=rows), :] = logit[:, t * 128 : (t + 1) * 128]
+            spun[pl.ds(place + k, tile, stride=chunk), :] = norm.astype(F32)
+
+    def turn(part, k):
+        other = lax.rem(r + k, rows_n)
+        return pltpu.make_async_remote_copy(
+            src_ref=ready.at[part, pl.ds(other * slab, slab)],
+            dst_ref=turned_ref.at[
+                :, pl.ds(pl.multiple_of(r * rows + part * chunk, chunk), chunk), :
+            ],
+            send_sem=turn_send.at[part, k],
+            recv_sem=turn_recv.at[part, r],
+            device_id=(other, c),
+            device_id_type=MESH,
+        )
+
+    def local_turn(part):
+        return pltpu.make_async_copy(
+            ready.at[part, pl.ds(r * slab, slab)],
+            turned_ref.at[:, pl.ds(pl.multiple_of(r * rows + part * chunk, chunk), chunk), :],
+            local_sem.at[part],
+        )
+
+    parts = rows // chunk
+    for part in range(parts):
+        @pl.loop(0, chunk // block)
+        def _(n):
+            do_block(part * chunk + n * block, n * block)
+
+        ready[part] = spun[...].astype(BF16).reshape(tile, chunk, lanes)
+        if part == 0:
+            pl.semaphore_wait(barrier, rows_n)
+        local_turn(part).start()
+
+        @pl.loop(1, rows_n)
+        def _(k):
+            turn(part, k).start()
+
+    logits = jnp.concatenate([lg[t] for t in range(tile // 128)], axis=1)
+    peak = jnp.max(logits, axis=-1, keepdims=True)
+    weights = jnp.exp(logits - peak).astype(BF16)
+    groups = 2
+    heads_in = heads // groups
+    gspan = heads_in * rows
+    glanes = value_ref.shape[1] // groups
+    each = glanes // heads_in
+
+    def pick(res):
+        lane = lax.broadcasted_iota(jnp.int32, (rows, glanes), 1)
+        total = res[:rows]
+        for h in range(1, heads_in):
+            total = jnp.where(lane >= h * each, res[h * rows : (h + 1) * rows], total)
+        return total
+
+    ones = jnp.ones((tile, glanes), BF16)
+    for g in range(groups):
+        stat[0, :, g * glanes : (g + 1) * glanes] = pick(
+            jnp.broadcast_to(peak[g * gspan : (g + 1) * gspan], (gspan, glanes))
+        )
+        stat[1, :, g * glanes : (g + 1) * glanes] = pick(
+            dot_nn(weights[g * gspan : (g + 1) * gspan], ones)
+        )
+
+    @pl.loop(0, half)
+    def _(s):
+        values = dot_nn(cols_ref[s], value_ref[...]).astype(BF16)
+        for g in range(groups):
+            num[s, :, g * glanes : (g + 1) * glanes] = pick(
+                dot_nn(
+                    weights[g * gspan : (g + 1) * gspan], values[:, g * glanes : (g + 1) * glanes]
+                )
+            )
+
+    mine = pl.ds(pl.multiple_of(c * slab, slab), slab)
+    theirs = pl.ds(pl.multiple_of((1 - c) * slab, slab), slab)
+    nsend[...] = num[:, theirs, :].astype(BF16)
+    ssend[...] = stat[:, theirs, :]
+    swaps = []
+    for n, (src, dst) in enumerate(((nsend, nrecv), (ssend, srecv))):
+        swap = pltpu.make_async_remote_copy(
+            src_ref=src, dst_ref=dst, send_sem=col_send.at[n], recv_sem=col_recv.at[n],
+            device_id=(r, 1 - c), device_id_type=MESH,
+        )
+        swap.start()
+        swaps.append(swap)
+    for swap in swaps:
+        swap.wait()
+    own_stat = stat[:, mine, :]
+    got_stat = srecv[...]
+    top = jnp.maximum(own_stat[0], got_stat[0])
+    own_scale = jnp.exp(own_stat[0] - top)
+    got_scale = jnp.exp(got_stat[0] - top)
+    inverse = 1.0 / (own_scale * own_stat[1] + got_scale * got_stat[1])
+    own_scale = (own_scale * inverse)[None]
+    got_scale = (got_scale * inverse)[None]
+    wide_lanes = num.shape[2]
+    step = 8
+
+    @pl.loop(0, half // step)
+    def _(n):
+        part = pl.ds(n * step, step)
+        norm = rows_ref[part, mine, :].reshape(step * slab, lanes)
+        gate = jax.nn.sigmoid(dot_nn(norm, gate_ref[...]))
+        mixed = own_scale * num[part, mine, :] + got_scale * nrecv[part].astype(F32)
+        gated = gate * mixed.reshape(step * slab, wide_lanes)
+        high = gated.astype(BF16)
+        low = (gated - high.astype(F32)).astype(BF16)
+        res = (dot_nn(high, out_ref[...]) + dot_nn(low, out_ref[...])).astype(BF16)
+        res = res.reshape(step, slab, lanes)
+        update_ref[part] = res[:, :, : lanes // 2]
+        update_ref[pl.ds(half + n * step, step)] = res[:, :, lanes // 2 :]
+
+    for part in range(parts):
+        @pl.loop(1, rows_n)
+        def _(k):
+            turn(part, k).wait_send()
+            source = lax.rem(r + k, rows_n)
+            pltpu.make_async_remote_copy(
+                src_ref=ready.at[part, pl.ds(0, slab)],
+                dst_ref=turned_ref.at[
+                    :, pl.ds(pl.multiple_of(source * rows + part * chunk, chunk), chunk), :
+                ],
+                send_sem=turn_send.at[part, k],
+                recv_sem=turn_recv.at[part, source],
+                device_id=(source, c),
+                device_id_type=MESH,
+            ).wait_recv()
+
+        local_turn(part).wait()
+
+
+def triangle_kernel(split_at, turned_ref, proj_ref, bias_ref, inputs_ref, edge_ref, edges):
+    j = pl.program_id(0)
+    slab = edge_ref.shape[1]
+    block = turned_ref[0]
+    projected = dot_nn(block, proj_ref[...])
+    inputs_ref[0, :, :split_at] = projected[:, :split_at].astype(BF16)
+    inputs_ref[0, :, split_at:] = jax.nn.sigmoid(projected[:, split_at:]).astype(BF16)
+    padded = bias_ref.shape[0]
+    bias_rows = dot_nt(bias_ref[...], block)
+    for t in range(edges.shape[0]):
+        edges.at[t][pl.ds(j, padded, stride=slab), :] = bias_rows[:, t * 128 : (t + 1) * 128]
+
+    @pl.when(j == slab - 1)
+    def _():
+        for t in range(edges.shape[0]):
+            kept = edges[t, : edge_ref.shape[0] * slab].astype(BF16)
+            edge_ref[:, :, t * 128 : (t + 1) * 128] = kept.reshape(edge_ref.shape[:2] + (128,))
+
+
+def two_fold(weight):
+    zero = jnp.zeros_like(weight)
+    return jnp.concatenate(
+        [jnp.concatenate([weight, zero], axis=1), jnp.concatenate([zero, weight], axis=1)], axis=0
+    )
+
+
+def head_fold(weight, heads):
+    width = weight.shape[1] // heads
+    split = weight.reshape(weight.shape[0], heads, 1, width)
+    zero = jnp.zeros_like(split)
+    top = jnp.concatenate([split, zero], axis=2)
+    low = jnp.concatenate([zero, split], axis=2)
+    return jnp.concatenate([top, low], axis=0).reshape(2 * weight.shape[0], 2 * weight.shape[1])
+
+
+def fast_device(
+    alignment, pair_rep, outer_left, outer_right, outer_proj, outer_bias, average_value,
+    average_gate, average_logit, average_out, triangle_proj, triangle_bias,
+):
+    rows_n = lax.axis_size("row")
+    seqs, slab, channels = alignment.shape
+    rows, tile, width = pair_rep.shape
+    factor = outer_left.shape[1]
+    heads = average_logit.shape[1]
+    half = seqs // 2
+    lanes = 2 * channels
+    full = 2 * average_value.shape[1]
+    vmem = pl.BlockSpec(memory_space=pltpu.VMEM)
+    limit = 56 * 1024 * 1024
+    dma = pltpu.SemaphoreType.DMA
+    cols, row_norm = pl.pallas_call(
+        functools.partial(gather_kernel, rows_n),
+        out_shape=(
+            jax.ShapeDtypeStruct((half, tile, lanes), BF16),
+            jax.ShapeDtypeStruct((half, rows, lanes), BF16),
+        ),
+        in_specs=[vmem],
+        out_specs=(vmem, vmem),
+        scratch_shapes=[
+            pltpu.VMEM((half, slab, lanes), BF16),
+            dma((rows_n,)),
+            dma((rows_n,)),
+            dma((2,)),
+        ],
+        compiler_params=pltpu.CompilerParams(
+            collective_id=0, has_side_effects=True, vmem_limit_bytes=limit
+        ),
+    )(alignment)
+    scaled = outer_proj.reshape(factor, factor, width).transpose(2, 1, 0)
+    scaled = scaled.reshape(width, factor * factor) * (1.0 / seqs)
+    pair_new, alignment_update, turned = pl.pallas_call(
+        functools.partial(pair_kernel, rows_n, heads),
+        out_shape=(
+            jax.ShapeDtypeStruct(pair_rep.shape, BF16),
+            jax.ShapeDtypeStruct(alignment.shape, BF16),
+            jax.ShapeDtypeStruct((slab, rows_n * rows, width), BF16),
+        ),
+        in_specs=[vmem] * 11,
+        out_specs=(vmem, vmem, vmem),
+        scratch_shapes=[
+            pltpu.VMEM((tile // 128, seqs * factor, 128), F32),
+            pltpu.VMEM((seqs, factor * tile), BF16),
+            pltpu.VMEM((half * rows, lanes), F32),
+            pltpu.VMEM((rows * factor, seqs), BF16),
+            pltpu.VMEM((8, factor * factor, tile), BF16),
+            pltpu.VMEM((tile * slab, width), F32),
+            pltpu.VMEM((rows // slab, tile, slab, width), BF16),
+            pltpu.VMEM((tile // 128, heads * rows, 128), F32),
+            pltpu.VMEM((half, rows, full), F32),
+            pltpu.VMEM((2, rows, full), F32),
+            pltpu.VMEM((half, slab, full), BF16),
+            pltpu.VMEM((half, slab, full), BF16),
+            pltpu.VMEM((2, slab, full), F32),
+            pltpu.VMEM((2, slab, full), F32),
+            dma((rows // slab, rows_n)),
+            dma((rows // slab, rows_n)),
+            dma((rows // slab,)),
+            dma((2,)),
+            dma((2,)),
+        ],
+        compiler_params=pltpu.CompilerParams(
+            collective_id=1, has_side_effects=True, vmem_limit_bytes=limit
+        ),
+    )(
+        cols, row_norm, pair_rep, two_fold(outer_right.T), two_fold(outer_left.T), scaled,
+        outer_bias.reshape(1, -1), head_fold(average_value, heads), head_fold(average_gate, heads),
+        average_logit.T, head_fold(average_out.T, heads).T,
+    )
+    edge_heads = triangle_bias.shape[1]
+    edge_weight = jnp.pad(triangle_bias.T, ((0, 8 - edge_heads), (0, 0)))
+    total = rows_n * rows
+    split_at = 3 * (triangle_proj.shape[1] // 4)
+    triangle_inputs, edge_bias = pl.pallas_call(
+        functools.partial(triangle_kernel, split_at),
+        grid=(slab,),
+        out_shape=(
+            jax.ShapeDtypeStruct((slab, total, triangle_proj.shape[1]), BF16),
+            jax.ShapeDtypeStruct((edge_heads, slab, total), BF16),
+        ),
+        in_specs=[
+            pl.BlockSpec((1, total, width), lambda j: (j, 0, 0)),
+            pl.BlockSpec(triangle_proj.shape, lambda j: (0, 0)),
+            pl.BlockSpec(edge_weight.shape, lambda j: (0, 0)),
+        ],
+        out_specs=(
+            pl.BlockSpec((1, total, triangle_proj.shape[1]), lambda j: (j, 0, 0)),
+            pl.BlockSpec((edge_heads, slab, total), lambda j: (0, 0, 0)),
+        ),
+        scratch_shapes=[pltpu.VMEM((total // 128, 8 * slab, 128), F32)],
+        compiler_params=pltpu.CompilerParams(vmem_limit_bytes=limit),
+    )(turned, triangle_proj, edge_weight)
+    return (pair_new, alignment_update, triangle_inputs, edge_bias)
+
+
+def choose_device(alignment, pair_rep, *rest):
+    rows_n, cols_n = lax.axis_size("row"), lax.axis_size("col")
+    slab, rows, tile = alignment.shape[1], pair_rep.shape[0], pair_rep.shape[1]
+    fits = cols_n == 2 and rows_n % 4 == 0 and slab % 16 == 0 and rows == 2 * slab
+    fits = fits and tile == rows_n * slab and tile % 128 == 0
+    chosen = fast_device if fits else per_device
+    return chosen(alignment, pair_rep, *rest)
+
+
 def solution(mesh):
     placed = (
         P(None, ("col", "row"), None),
@@ -152,7 +623,7 @@
         P(),
     )
     return jax.shard_map(
-        per_device,
+        choose_device,
         mesh=mesh,
         in_specs=placed,
         out_specs=(

time: 262 us -> 125 us (0.48)
  the two profiles are of different devices: /device:TPU:0 before, /device:TPU:15 now
where the time goes in v1:
time: 125 us; the launch traced here: 124 us
  Pallas kernels  113 us (90%)
  local copies, waits for them, and re-layouts  9.15 us (7%)
  other arithmetic  1.77 us (1%)
    pallas_call x1, Pallas kernels, fast_device(): pl.pallas_call(functools.partial(pair_kernel, rows_n, heads), out_shape=(...  75.3 us
    pallas_call x1, Pallas kernels, fast_device(): pl.pallas_call(functools.partial(gather_kernel, rows_n), out_shape=(jax.S...  24.6 us
    pallas_call x1, Pallas kernels, fast_device(): pl.pallas_call(functools.partial(triangle_kernel, split_at), grid=(slab,)...  12.6 us
    unnamed x11, local copies, waits for them, and re-layouts  4.64 us

profile of v1, /device:TPU:15, one launch (start us, length us, event | category | flops | bytes accessed | tf_op | source)
XLA Modules:
  0.0 124.2 jit_solution(17750286475571069739)
XLA Ops:
  0.6 0.0 copy-start.1
  0.6 1.3 %pad.14.bias_ref = bf16[8,128]{1,0:T(8,128)(2,1)} pad(bf16[4,128]{1,0:T(4,128)(2,1)} %bitcast.30, bf16[]{:T(256)} %constant.2.clone.1), padding=0_4x0_0 | pad | bytes 3074 | tf_op jit(solution)/shard_map/jit(_pad)/pad | solution.py:576
  2.0 1.5 %fusion.13 = (bf16[64,128]{1,0:T(8,128)(2,1)}, bf16[64,128]{1,0:T(8,128)(2,1)}) fusion(bf16[32,64]{1,0:T(8,128)(2,1)} %bitcast.27, bf16[32,64]{1,0:T(8,128)(2,1)} %bitcast.28), kind=kLoop, calls=%fused_computation.18 | loop fusion | flops 114688 | bytes 40960 | tf_op jit(solution)/shard_map/concatenate | solution.py:488
  3.4 0.9 copy.33
  4.3 0.1 fusion.6
  4.4 0.8 copy.40.value_ref
  5.2 0.9 copy.35
  6.1 0.1 fusion.7
  6.2 0.8 copy.41.gate_ref
  7.0 0.9 copy.37
  7.8 0.1 fusion.8
  7.9 0.7 copy.38
  8.6 0.0 copy-done.1
  8.6 0.1 copy.32
  8.7 0.9 copy.39.proj_ref
  9.6 24.6 %shard_map.147 = (bf16[32,256,128]{2,1,0:T(8,128)(2,1)}, bf16[32,32,128]{2,1,0:T(8,128)(2,1)}) custom-call(bf16[64,16,64]{2,1,0:T(8,128)(2,1)} %align_ref.1), custom_call_target="tpu_custom_call" | custom-call | tf_op jit(solution)/shard_map/pallas_call | solution.py:517
  34.2 75.3 %shard_map.148 = (bf16[32,256,128]{2,1,0:T(8,128)(2,1)}, bf16[64,16,64]{2,1,0:T(8,128)(2,1)}, bf16[16,512,128]{2,1,0:T(8,128)(2,1)}) custom-call(bf16[32,256,128]{2,1,0:T(8,128)(2,1)} %get-tuple-element.11.cols_ref, bf16[32,32,128]{2,1,0:T(8,128)(2,1)} %get-tuple-element.12.rows_ref, bf16[32,256,128]{2,1,0:T(8,128)(2,1)} %pair_ref.1, ...), custom_call_target="tpu_custom_call" | custom-call | tf_op jit(solution)/shard_map/pallas_call | solution.py:537
  109.5 0.0 copy-start
  109.5 12.6 %shard_map.149 = (bf16[16,512,512]{2,1,0:T(8,128)(2,1)}, bf16[4,16,512]{2,1,0:T(8,128)(2,1)}) custom-call(bf16[16,512,128]{2,1,0:T(8,128)(2,1)} %get-tuple-element.15.turned_ref, bf16[128,512]{1,0:T(8,128)(2,1)} %proj_ref.1, bf16[8,128]{1,0:T(8,128)(2,1)} %pad.14.bias_ref), custom_call_target="tpu_custom_call" | custom-call | tf_op jit(solution)/shard_map/pallas_call | solution.py:579
  122.1 0.0 copy-done
  122.1 0.0 copy-start.2
  122.1 1.3 %copy.44 = bf16[32,256,128]{2,1,0:T(8,128)(2,1)} copy(bf16[32,256,128]{2,1,0:T(8,128)(2,1)S(1)} %copy-done) | data formatting | bytes 4194304
  123.4 0.0 copy-done.2
  123.4 0.7 copy.45
  (3 shorter events, 0.0 us)
Async XLA Ops:
  0.6 8.0 %copy-start.1 = (bf16[1024,128]{1,0:T(8,128)(2,1)S(1)}, bf16[1024,128]{1,0:T(8,128)(2,1)}, u32[]{:S(2)}) copy-start(bf16[1024,128]{1,0:T(8,128)(2,1)} %param.16) | copy-start | bytes 786436
  109.5 12.7 %copy-start = (bf16[32,256,128]{2,1,0:T(8,128)(2,1)S(1)}, bf16[32,256,128]{2,1,0:T(8,128)(2,1)}, u32[]{:S(2)}) copy-start(bf16[32,256,128]{2,1,0:T(8,128)(2,1)} %get-tuple-element.24) | copy-start | bytes 6291460
  122.1 1.3 %copy-start.2 = (bf16[64,16,64]{2,1,0:T(8,128)(2,1)S(1)}, bf16[64,16,64]{2,1,0:T(8,128)(2,1)}, u32[]{:S(2)}) copy-start(bf16[64,16,64]{2,1,0:T(8,128)(2,1)} %get-tuple-element.25) | copy-start | bytes 393220

commit v2 on v1

--- a/solution.py
+++ b/solution.py
@@ -152,8 +152,27 @@
     return jnp.dot(a, b, preferred_element_type=F32)
 
 
-def gather_kernel(rows_n, align_ref, cols_ref, rows_ref, own, send_sem, recv_sem, row_sem):
-    half, slab = own.shape[0], own.shape[1]
+def two_fold(weight, ref):
+    wide = weight.astype(F32)
+    zero = jnp.zeros_like(wide)
+    tall, across = weight.shape
+    ref[:tall] = jnp.concatenate([wide, zero], axis=1).astype(BF16)
+    ref[tall:] = jnp.concatenate([zero, wide], axis=1).astype(BF16)
+
+
+def fused_kernel(
+    rows_n, heads, align_ref, pair_hbm, right_ref, left_ref, proj_ref, bias_ref, value_ref,
+    gate_ref, logit_ref, out_ref, new_ref, update_ref, turned_ref, own, cols_ref, rows_ref,
+    pair_ref, fresh_ref, right_w, left_w, value_w, gate_w, out_w, proj_wide, proj_back, proj_w,
+    rs, rb, nr, lt, outer, spun, ready, lg, num, stat, nsend, nrecv, ssend, srecv, send_sem,
+    recv_sem, row_sem, turn_send, turn_recv, local_sem, col_send, col_recv,
+):
+    half, tile, lanes = cols_ref.shape
+    rows = rows_ref.shape[1]
+    slab = tile // rows_n
+    width = right_ref.shape[0]
+    block = 8
+    chunk = slab
     r, c = lax.axis_index("row"), lax.axis_index("col")
     far = rows_n // 4
     a, b, e = r // 4, (r // 2) % 2, r % 2
@@ -169,8 +188,16 @@
     source_col = (2 * r) // rows_n
     source_row = lax.rem(2 * r, rows_n)
     barrier = pltpu.get_barrier_semaphore()
-    for spot in distant + [across, beside]:
-        pl.semaphore_signal(barrier, inc=1, device_id=place(*spot), device_id_type=MESH)
+    pair_load = pltpu.make_async_copy(pair_hbm, pair_ref, local_sem.at[0])
+    pair_load.start()
+
+    @pl.loop(1, rows_n)
+    def _(k):
+        pl.semaphore_signal(
+            barrier, inc=1, device_id=(lax.rem(r + k, rows_n), c), device_id_type=MESH
+        )
+
+    pl.semaphore_signal(barrier, inc=1, device_id=(r, 1 - c), device_id_type=MESH)
 
     @pl.when(source_col != c)
     def _():
@@ -184,7 +211,7 @@
     spread = jnp.mean(centered * centered, axis=-1, keepdims=True)
     norm = centered * lax.rsqrt(spread + 1e-05)
     own[...] = jnp.concatenate([norm[:half], norm[half:]], axis=-1).astype(BF16)
-    pl.semaphore_wait(barrier, far + 2)
+    pl.semaphore_wait(barrier, rows_n + 1)
 
     def window(index):
         return cols_ref.at[:, pl.ds(pl.multiple_of(index * slab, slab), slab), :]
@@ -228,6 +255,16 @@
     row_copy.start()
     started.append(row_copy)
     window(r)[...] = own[...]
+    two_fold(right_ref[...], right_w)
+    two_fold(left_ref[...], left_w)
+    two_fold(value_ref[...], value_w)
+    two_fold(gate_ref[...], gate_w)
+    two_fold(out_ref[...], out_w)
+    proj_wide[...] = proj_ref[...].astype(F32) * (1.0 / (2 * half))
+    for d in range(width):
+        turned_rows = proj_wide[pl.ds(d, width, stride=width), :]
+        proj_back[d * width : (d + 1) * width, :] = turned_rows
+    proj_w[...] = proj_back[...].T.astype(BF16)
 
     def index_of(spot):
         return spot[0] * 4 + spot[1] * 2 + spot[2]
@@ -267,36 +304,9 @@
                 device_id_type=MESH,
             ).wait_recv()
 
-    for copy in started:
-        copy.wait_send()
-
-
-def pair_kernel(
-    rows_n, heads, cols_ref, rows_ref, pair_ref, right_ref, left_ref, proj_ref, bias_ref, value_ref,
-    gate_ref, logit_ref, out_ref, new_ref, update_ref, turned_ref, rs, rb, nr, lt, outer, spun, ready,
-    lg, num, stat, nsend, nrecv, ssend, srecv, turn_send, turn_recv, local_sem, col_send, col_recv,
-):
-    half, tile, lanes = cols_ref.shape
-    rows = rows_ref.shape[1]
-    slab = tile // rows_n
-    width = right_ref.shape[0] // 2
-    block = 8
-    chunk = slab
-    span = heads * rows
-    r, c = lax.axis_index("row"), lax.axis_index("col")
-    barrier = pltpu.get_barrier_semaphore()
-
-    @pl.loop(1, rows_n)
-    def _(k):
-        pl.semaphore_signal(
-            barrier, inc=1, device_id=(lax.rem(r + k, rows_n), c), device_id_type=MESH
-        )
-
-    pl.semaphore_signal(barrier, inc=1, device_id=(r, 1 - c), device_id_type=MESH)
-
-    @pl.loop(0, half)
+    @pl.loop(0, half, unroll=8)
     def _(s):
-        res = dot_nt(right_ref[...], cols_ref[s])
+        res = dot_nt(right_w[...], cols_ref[s])
         for t in range(tile // 128):
             piece = res[:, t * 128 : (t + 1) * 128]
             rs[t, pl.ds(pl.multiple_of(s * width, width), width), :] = piece[:width]
@@ -308,12 +318,17 @@
             rb[:, at : at + 128] = rs.at[t][pl.ds(d, 2 * half, stride=width), :].astype(BF16)
 
     nr[...] = rows_ref[...].astype(F32).reshape(half * rows, lanes)
+    tokens = jnp.concatenate(
+        [nr[pl.ds(i, half, stride=rows), :].astype(BF16) for i in range(rows)], axis=0
+    )
+    left_all = dot_nt(left_w[...], tokens)
     for i in range(rows):
-        token = nr[pl.ds(i, half, stride=rows), :].astype(BF16)
-        res = dot_nt(left_ref[...], token)
+        res = left_all[:, i * half : (i + 1) * half]
         lt[i * width : (i + 1) * width, :] = jnp.concatenate(
             [res[:width], res[width:]], axis=1
         ).astype(BF16)
+
+    pair_load.wait()
 
     def do_block(base, place):
         left = lt[pl.ds(pl.multiple_of(base * width, block * width), block * width), :]
@@ -321,12 +336,11 @@
             res = dot_nn(left, rb[:, d * tile : (d + 1) * tile]).astype(BF16)
             outer[:, d * width : (d + 1) * width, :] = res.reshape(block, width, tile)
 
-        @pl.loop(0, block)
-        def _(k):
+        for k in range(block):
             i = base + k
-            update = dot_nn(proj_ref[...], outer[k]).T
+            update = dot_nn(proj_w[...], outer[k]).T
             fresh = (pair_ref[i].astype(F32) + update + bias_ref[...]).astype(BF16)
-            new_ref[i] = fresh
+            fresh_ref[i] = fresh
             wide = fresh.astype(F32)
             centered = wide - jnp.mean(wide, axis=-1, keepdims=True)
             spread = jnp.mean(centered * centered, axis=-1, keepdims=True)
@@ -353,7 +367,7 @@
         return pltpu.make_async_copy(
             ready.at[part, pl.ds(r * slab, slab)],
             turned_ref.at[:, pl.ds(pl.multiple_of(r * rows + part * chunk, chunk), chunk), :],
-            local_sem.at[part],
+            local_sem.at[1 + part],
         )
 
     parts = rows // chunk
@@ -363,48 +377,50 @@
             do_block(part * chunk + n * block, n * block)
 
         ready[part] = spun[...].astype(BF16).reshape(tile, chunk, lanes)
-        if part == 0:
-            pl.semaphore_wait(barrier, rows_n)
         local_turn(part).start()
 
         @pl.loop(1, rows_n)
         def _(k):
             turn(part, k).start()
 
+    new_store = pltpu.make_async_copy(fresh_ref, new_ref, local_sem.at[0])
+    new_store.start()
     logits = jnp.concatenate([lg[t] for t in range(tile // 128)], axis=1)
     peak = jnp.max(logits, axis=-1, keepdims=True)
     weights = jnp.exp(logits - peak).astype(BF16)
     groups = 2
     heads_in = heads // groups
     gspan = heads_in * rows
-    glanes = value_ref.shape[1] // groups
-    each = glanes // heads_in
+    wide_lanes = num.shape[2]
+    glanes = wide_lanes // groups
+    part_lanes = glanes // 2
+    each = part_lanes // heads_in
 
     def pick(res):
-        lane = lax.broadcasted_iota(jnp.int32, (rows, glanes), 1)
+        lane = lax.broadcasted_iota(jnp.int32, (rows, glanes), 1) % part_lanes
         total = res[:rows]
         for h in range(1, heads_in):
             total = jnp.where(lane >= h * each, res[h * rows : (h + 1) * rows], total)
         return total
 
+    def spots(g):
+        return [(g * part_lanes, 0), (wide_lanes // 2 + g * part_lanes, part_lanes)]
+
+    def put(ref, index, g, res):
+        for at, start in spots(g):
+            ref[index, :, at : at + part_lanes] = res[:, start : start + part_lanes]
+
     ones = jnp.ones((tile, glanes), BF16)
     for g in range(groups):
-        stat[0, :, g * glanes : (g + 1) * glanes] = pick(
-            jnp.broadcast_to(peak[g * gspan : (g + 1) * gspan], (gspan, glanes))
-        )
-        stat[1, :, g * glanes : (g + 1) * glanes] = pick(
-            dot_nn(weights[g * gspan : (g + 1) * gspan], ones)
-        )
-
-    @pl.loop(0, half)
+        put(stat, 0, g, pick(jnp.broadcast_to(peak[g * gspan : (g + 1) * gspan], (gspan, glanes))))
+        put(stat, 1, g, pick(dot_nn(weights[g * gspan : (g + 1) * gspan], ones)))
+
+    @pl.loop(0, half, unroll=4)
     def _(s):
-        values = dot_nn(cols_ref[s], value_ref[...]).astype(BF16)
+        values = dot_nn(cols_ref[s], value_w[...]).astype(BF16)
         for g in range(groups):
-            num[s, :, g * glanes : (g + 1) * glanes] = pick(
-                dot_nn(
-                    weights[g * gspan : (g + 1) * gspan], values[:, g * glanes : (g + 1) * glanes]
-                )
-            )
+            chosen = jnp.concatenate([values[:, at : at + part_lanes] for at, _ in spots(g)], axis=1)
+            put(num, s, g, pick(dot_nn(weights[g * gspan : (g + 1) * gspan], chosen)))
 
     mine = pl.ds(pl.multiple_of(c * slab, slab), slab)
     theirs = pl.ds(pl.multiple_of((1 - c) * slab, slab), slab)
@@ -428,19 +444,18 @@
     inverse = 1.0 / (own_scale * own_stat[1] + got_scale * got_stat[1])
     own_scale = (own_scale * inverse)[None]
     got_scale = (got_scale * inverse)[None]
-    wide_lanes = num.shape[2]
     step = 8
 
     @pl.loop(0, half // step)
     def _(n):
         part = pl.ds(n * step, step)
         norm = rows_ref[part, mine, :].reshape(step * slab, lanes)
-        gate = jax.nn.sigmoid(dot_nn(norm, gate_ref[...]))
+        gate = jax.nn.sigmoid(dot_nn(norm, gate_w[...]))
         mixed = own_scale * num[part, mine, :] + got_scale * nrecv[part].astype(F32)
         gated = gate * mixed.reshape(step * slab, wide_lanes)
         high = gated.astype(BF16)
         low = (gated - high.astype(F32)).astype(BF16)
-        res = (dot_nn(high, out_ref[...]) + dot_nn(low, out_ref[...])).astype(BF16)
+        res = (dot_nt(high, out_w[...]) + dot_nt(low, out_w[...])).astype(BF16)
         res = res.reshape(step, slab, lanes)
         update_ref[part] = res[:, :, : lanes // 2]
         update_ref[pl.ds(half + n * step, step)] = res[:, :, lanes // 2 :]
@@ -462,41 +477,31 @@
             ).wait_recv()
 
         local_turn(part).wait()
+    new_store.wait()
+    for copy in started:
+        copy.wait_send()
 
 
 def triangle_kernel(split_at, turned_ref, proj_ref, bias_ref, inputs_ref, edge_ref, edges):
     j = pl.program_id(0)
     slab = edge_ref.shape[1]
-    block = turned_ref[0]
-    projected = dot_nn(block, proj_ref[...])
-    inputs_ref[0, :, :split_at] = projected[:, :split_at].astype(BF16)
-    inputs_ref[0, :, split_at:] = jax.nn.sigmoid(projected[:, split_at:]).astype(BF16)
-    padded = bias_ref.shape[0]
-    bias_rows = dot_nt(bias_ref[...], block)
-    for t in range(edges.shape[0]):
-        edges.at[t][pl.ds(j, padded, stride=slab), :] = bias_rows[:, t * 128 : (t + 1) * 128]
-
-    @pl.when(j == slab - 1)
+    group = turned_ref.shape[0]
+    edge_heads = bias_ref.shape[0]
+    for n in range(group):
+        block = turned_ref[n]
+        projected = dot_nn(block, proj_ref[...])
+        inputs_ref[n, :, :split_at] = projected[:, :split_at].astype(BF16)
+        inputs_ref[n, :, split_at:] = jax.nn.sigmoid(projected[:, split_at:]).astype(BF16)
+        bias_rows = dot_nt(bias_ref[...], block)
+        for t in range(edges.shape[0]):
+            piece = bias_rows[:, t * 128 : (t + 1) * 128]
+            edges.at[t][pl.ds(j * group + n, edge_heads, stride=slab), :] = piece
+
+    @pl.when(j == slab // group - 1)
     def _():
         for t in range(edges.shape[0]):
             kept = edges[t, : edge_ref.shape[0] * slab].astype(BF16)
             edge_ref[:, :, t * 128 : (t + 1) * 128] = kept.reshape(edge_ref.shape[:2] + (128,))
-
-
-def two_fold(weight):
-    zero = jnp.zeros_like(weight)
-    return jnp.concatenate(
-        [jnp.concatenate([weight, zero], axis=1), jnp.concatenate([zero, weight], axis=1)], axis=0
-    )
-
-
-def head_fold(weight, heads):
-    width = weight.shape[1] // heads
-    split = weight.reshape(weight.shape[0], heads, 1, width)
-    zero = jnp.zeros_like(split)
-    top = jnp.concatenate([split, zero], axis=2)
-    low = jnp.concatenate([zero, split], axis=2)
-    return jnp.concatenate([top, low], axis=0).reshape(2 * weight.shape[0], 2 * weight.shape[1])
 
 
 def fast_device(
@@ -514,43 +519,38 @@
     vmem = pl.BlockSpec(memory_space=pltpu.VMEM)
     limit = 56 * 1024 * 1024
     dma = pltpu.SemaphoreType.DMA
-    cols, row_norm = pl.pallas_call(
-        functools.partial(gather_kernel, rows_n),
-        out_shape=(
-            jax.ShapeDtypeStruct((half, tile, lanes), BF16),
-            jax.ShapeDtypeStruct((half, rows, lanes), BF16),
-        ),
-        in_specs=[vmem],
-        out_specs=(vmem, vmem),
-        scratch_shapes=[
-            pltpu.VMEM((half, slab, lanes), BF16),
-            dma((rows_n,)),
-            dma((rows_n,)),
-            dma((2,)),
-        ],
-        compiler_params=pltpu.CompilerParams(
-            collective_id=0, has_side_effects=True, vmem_limit_bytes=limit
-        ),
-    )(alignment)
-    scaled = outer_proj.reshape(factor, factor, width).transpose(2, 1, 0)
-    scaled = scaled.reshape(width, factor * factor) * (1.0 / seqs)
+    anywhere = pl.BlockSpec(memory_space=pl.ANY)
+    parts = rows // slab
     pair_new, alignment_update, turned = pl.pallas_call(
-        functools.partial(pair_kernel, rows_n, heads),
+        functools.partial(fused_kernel, rows_n, heads),
         out_shape=(
             jax.ShapeDtypeStruct(pair_rep.shape, BF16),
             jax.ShapeDtypeStruct(alignment.shape, BF16),
             jax.ShapeDtypeStruct((slab, rows_n * rows, width), BF16),
         ),
-        in_specs=[vmem] * 11,
-        out_specs=(vmem, vmem, vmem),
+        in_specs=[vmem, anywhere] + [vmem] * 8,
+        out_specs=(anywhere, vmem, anywhere),
         scratch_shapes=[
+            pltpu.VMEM((half, slab, lanes), BF16),
+            pltpu.VMEM((half, tile, lanes), BF16),
+            pltpu.VMEM((half, rows, lanes), BF16),
+            pltpu.VMEM(pair_rep.shape, BF16),
+            pltpu.VMEM(pair_rep.shape, BF16),
+            pltpu.VMEM((2 * factor, lanes), BF16),
+            pltpu.VMEM((2 * factor, lanes), BF16),
+            pltpu.VMEM((lanes, full), BF16),
+            pltpu.VMEM((lanes, full), BF16),
+            pltpu.VMEM((lanes, full), BF16),
+            pltpu.VMEM((factor * factor, width), F32),
+            pltpu.VMEM((factor * factor, width), F32),
+            pltpu.VMEM((width, factor * factor), BF16),
             pltpu.VMEM((tile // 128, seqs * factor, 128), F32),
             pltpu.VMEM((seqs, factor * tile), BF16),
             pltpu.VMEM((half * rows, lanes), F32),
             pltpu.VMEM((rows * factor, seqs), BF16),
             pltpu.VMEM((8, factor * factor, tile), BF16),
             pltpu.VMEM((tile * slab, width), F32),
-            pltpu.VMEM((rows // slab, tile, slab, width), BF16),
+            pltpu.VMEM((parts, tile, slab, width), BF16),
             pltpu.VMEM((tile // 128, heads * rows, 128), F32),
             pltpu.VMEM((half, rows, full), F32),
             pltpu.VMEM((2, rows, full), F32),
@@ -558,41 +558,44 @@
             pltpu.VMEM((half, slab, full), BF16),
             pltpu.VMEM((2, slab, full), F32),
             pltpu.VMEM((2, slab, full), F32),
-            dma((rows // slab, rows_n)),
-            dma((rows // slab, rows_n)),
-            dma((rows // slab,)),
+            dma((rows_n,)),
+            dma((rows_n,)),
+            dma((2,)),
+            dma((parts, rows_n)),
+            dma((parts, rows_n)),
+            dma((1 + parts,)),
             dma((2,)),
             dma((2,)),
         ],
         compiler_params=pltpu.CompilerParams(
-            collective_id=1, has_side_effects=True, vmem_limit_bytes=limit
+            collective_id=0, has_side_effects=True, vmem_limit_bytes=limit
         ),
     )(
-        cols, row_norm, pair_rep, two_fold(outer_right.T), two_fold(outer_left.T), scaled,
-        outer_bias.reshape(1, -1), head_fold(average_value, heads), head_fold(average_gate, heads),
-        average_logit.T, head_fold(average_out.T, heads).T,
+        alignment, pair_rep, outer_right.T, outer_left.T, outer_proj, outer_bias.reshape(1, -1),
+        average_value, average_gate, average_logit.T, average_out.T,
     )
     edge_heads = triangle_bias.shape[1]
-    edge_weight = jnp.pad(triangle_bias.T, ((0, 8 - edge_heads), (0, 0)))
+    edge_weight = triangle_bias.T
+    group = 4
     total = rows_n * rows
     split_at = 3 * (triangle_proj.shape[1] // 4)
     triangle_inputs, edge_bias = pl.pallas_call(
         functools.partial(triangle_kernel, split_at),
-        grid=(slab,),
+        grid=(slab // group,),
         out_shape=(
             jax.ShapeDtypeStruct((slab, total, triangle_proj.shape[1]), BF16),
             jax.ShapeDtypeStruct((edge_heads, slab, total), BF16),
         ),
         in_specs=[
-            pl.BlockSpec((1, total, width), lambda j: (j, 0, 0)),
+            pl.BlockSpec((group, total, width), lambda j: (j, 0, 0)),
             pl.BlockSpec(triangle_proj.shape, lambda j: (0, 0)),
             pl.BlockSpec(edge_weight.shape, lambda j: (0, 0)),
         ],
         out_specs=(
-            pl.BlockSpec((1, total, triangle_proj.shape[1]), lambda j: (j, 0, 0)),
+            pl.BlockSpec((group, total, triangle_proj.shape[1]), lambda j: (j, 0, 0)),
             pl.BlockSpec((edge_heads, slab, total), lambda j: (0, 0, 0)),
         ),
-        scratch_shapes=[pltpu.VMEM((total // 128, 8 * slab, 128), F32)],
+        scratch_shapes=[pltpu.VMEM((total // 128, edge_heads * slab, 128), F32)],
         compiler_params=pltpu.CompilerParams(vmem_limit_bytes=limit),
     )(turned, triangle_proj, edge_weight)
     return (pair_new, alignment_update, triangle_inputs, edge_bias)
@@ -602,7 +605,8 @@
     rows_n, cols_n = lax.axis_size("row"), lax.axis_size("col")
     slab, rows, tile = alignment.shape[1], pair_rep.shape[0], pair_rep.shape[1]
     fits = cols_n == 2 and rows_n % 4 == 0 and slab % 16 == 0 and rows == 2 * slab
-    fits = fits and tile == rows_n * slab and tile % 128 == 0
+    seqs = alignment.shape[0]
+    fits = fits and tile == rows_n * slab and tile % 128 == 0 and seqs & (seqs - 1) == 0
     chosen = fast_device if fits else per_device
     return chosen(alignment, pair_rep, *rest)
 

time: 125 us -> 98.4 us (0.79)
  the two profiles are of different devices: /device:TPU:15 before, /device:TPU:31 now
where the time goes in v2:
time: 98.4 us; the launch traced here: 98.2 us
  Pallas kernels  95.5 us (97%)
  local copies, waits for them, and re-layouts  2.03 us (2%)
    pallas_call x1, Pallas kernels, fast_device(): pl.pallas_call(functools.partial(fused_kernel, rows_n, heads), out_shape=...  88.6 us
    pallas_call x1, Pallas kernels, fast_device(): pl.pallas_call(functools.partial(triangle_kernel, split_at), grid=(slab /...  6.89 us
    unnamed x6, local copies, waits for them, and re-layouts  2.03 us

profile of v2, /device:TPU:31, one launch (start us, length us, event | category | flops | bytes accessed | tf_op | source)
XLA Modules:
  0.0 98.2 jit_solution(14663056496609364271)
XLA Ops:
  0.6 88.6 %shard_map.147 = (bf16[32,256,128]{2,1,0:T(8,128)(2,1)}, bf16[64,16,64]{2,1,0:T(8,128)(2,1)}, bf16[16,512,128]{2,1,0:T(8,128)(2,1)}) custom-call(bf16[64,16,64]{2,1,0:T(8,128)(2,1)} %align_ref.1, bf16[32,256,128]{2,1,0:T(8,128)(2,1)} %pair_hbm.1, bf16[32,64]{1,0:T(8,128)(2,1)} %bitcast.7, bf16[32,64]{1,0:T(8,128)(2,1)} %bitcast.8, ...), custom_call_target="tpu_custom_call" | custom-call | tf_op jit(solution)/shard_map/pallas_call | solution.py:524
  89.2 0.0 copy-start
  89.3 6.9 %shard_map.148 = (bf16[16,512,512]{2,1,0:T(8,128)(2,1)}, bf16[4,16,512]{2,1,0:T(8,128)(2,1)}) custom-call(bf16[16,512,128]{2,1,0:T(8,128)(2,1)} %get-tuple-element.11.turned_ref, bf16[128,512]{1,0:T(8,128)(2,1)} %proj_ref.3, bf16[4,128]{1,0:T(4,128)(2,1)} %bitcast.10), custom_call_target="tpu_custom_call" | custom-call | tf_op jit(solution)/shard_map/pallas_call | solution.py:582
  96.1 0.0 copy-done
  96.1 0.0 copy-start.1
  96.2 1.3 %copy.18 = bf16[32,256,128]{2,1,0:T(8,128)(2,1)} copy(bf16[32,256,128]{2,1,0:T(8,128)(2,1)S(1)} %copy-done) | data formatting | bytes 4194304
  97.5 0.0 copy-done.1
  97.5 0.7 copy.19
Async XLA Ops:
  89.2 6.9 %copy-start = (bf16[32,256,128]{2,1,0:T(8,128)(2,1)S(1)}, bf16[32,256,128]{2,1,0:T(8,128)(2,1)}, u32[]{:S(2)}) copy-start(bf16[32,256,128]{2,1,0:T(8,128)(2,1)} %get-tuple-element.18) | copy-start | bytes 6291460
  96.1 1.3 %copy-start.1 = (bf16[64,16,64]{2,1,0:T(8,128)(2,1)S(1)}, bf16[64,16,64]{2,1,0:T(8,128)(2,1)}, u32[]{:S(2)}) copy-start(bf16[64,16,64]{2,1,0:T(8,128)(2,1)} %get-tuple-element.19) | copy-start | bytes 393220

commit v3 on v2

--- a/solution.py
+++ b/solution.py
@@ -381,7 +381,7 @@
 
         @pl.loop(1, rows_n)
         def _(k):
-            turn(part, k).start()
+            turn(part, lax.rem(k + rows_n // 2 - 2, rows_n - 1) + 1).start()
 
     new_store = pltpu.make_async_copy(fresh_ref, new_ref, local_sem.at[0])
     new_store.start()
@@ -415,27 +415,36 @@
         put(stat, 0, g, pick(jnp.broadcast_to(peak[g * gspan : (g + 1) * gspan], (gspan, glanes))))
         put(stat, 1, g, pick(dot_nn(weights[g * gspan : (g + 1) * gspan], ones)))
 
-    @pl.loop(0, half, unroll=4)
-    def _(s):
-        values = dot_nn(cols_ref[s], value_w[...]).astype(BF16)
-        for g in range(groups):
-            chosen = jnp.concatenate([values[:, at : at + part_lanes] for at, _ in spots(g)], axis=1)
-            put(num, s, g, pick(dot_nn(weights[g * gspan : (g + 1) * gspan], chosen)))
-
     mine = pl.ds(pl.multiple_of(c * slab, slab), slab)
     theirs = pl.ds(pl.multiple_of((1 - c) * slab, slab), slab)
-    nsend[...] = num[:, theirs, :].astype(BF16)
-    ssend[...] = stat[:, theirs, :]
-    swaps = []
-    for n, (src, dst) in enumerate(((nsend, nrecv), (ssend, srecv))):
-        swap = pltpu.make_async_remote_copy(
+    step = 8
+
+    def swap(src, dst, n):
+        copy = pltpu.make_async_remote_copy(
             src_ref=src, dst_ref=dst, send_sem=col_send.at[n], recv_sem=col_recv.at[n],
             device_id=(r, 1 - c), device_id_type=MESH,
         )
-        swap.start()
-        swaps.append(swap)
-    for swap in swaps:
-        swap.wait()
+        copy.start()
+        return copy
+
+    ssend[...] = stat[:, theirs, :]
+    stat_swap = swap(ssend, srecv, half // step)
+    swaps = []
+    for n in range(half // step):
+        @pl.loop(n * step, (n + 1) * step, unroll=4)
+        def _(s):
+            values = dot_nn(cols_ref[s], value_w[...]).astype(BF16)
+            for g in range(groups):
+                chosen = jnp.concatenate(
+                    [values[:, at : at + part_lanes] for at, _ in spots(g)], axis=1
+                )
+                put(num, s, g, pick(dot_nn(weights[g * gspan : (g + 1) * gspan], chosen)))
+
+        part = pl.ds(n * step, step)
+        nsend[part] = num[part, theirs, :].astype(BF16)
+        swaps.append(swap(nsend.at[part], nrecv.at[part], n))
+
+    stat_swap.wait()
     own_stat = stat[:, mine, :]
     got_stat = srecv[...]
     top = jnp.maximum(own_stat[0], got_stat[0])
@@ -444,10 +453,9 @@
     inverse = 1.0 / (own_scale * own_stat[1] + got_scale * got_stat[1])
     own_scale = (own_scale * inverse)[None]
     got_scale = (got_scale * inverse)[None]
-    step = 8
-
-    @pl.loop(0, half // step)
-    def _(n):
+
+    for n in range(half // step):
+        swaps[n].wait()
         part = pl.ds(n * step, step)
         norm = rows_ref[part, mine, :].reshape(step * slab, lanes)
         gate = jax.nn.sigmoid(dot_nn(norm, gate_w[...]))
@@ -564,8 +572,8 @@
             dma((parts, rows_n)),
             dma((parts, rows_n)),
             dma((1 + parts,)),
-            dma((2,)),
-            dma((2,)),
+            dma((1 + half // 8,)),
+            dma((1 + half // 8,)),
         ],
         compiler_params=pltpu.CompilerParams(
             collective_id=0, has_side_effects=True, vmem_limit_bytes=limit

time: 98.4 us -> 99.7 us (1.013)
  the two profiles are of different devices: /device:TPU:31 before, /device:TPU:0 now
where the time goes in v3:
time: 99.7 us; the launch traced here: 99.5 us
  Pallas kernels  96.8 us (97%)
  local copies, waits for them, and re-layouts  2.03 us (2%)
    pallas_call x1, Pallas kernels, fast_device(): pl.pallas_call(functools.partial(fused_kernel, rows_n, heads), out_shape=...  89.9 us
    pallas_call x1, Pallas kernels, fast_device(): pl.pallas_call(functools.partial(triangle_kernel, split_at), grid=(slab /...  6.88 us
    unnamed x6, local copies, waits for them, and re-layouts  2.03 us

profile of v3, /device:TPU:0, one launch (start us, length us, event | category | flops | bytes accessed | tf_op | source)
XLA Modules:
  0.0 99.5 jit_solution(438813326439462063)
XLA Ops:
  0.6 89.9 %shard_map.147 = (bf16[32,256,128]{2,1,0:T(8,128)(2,1)}, bf16[64,16,64]{2,1,0:T(8,128)(2,1)}, bf16[16,512,128]{2,1,0:T(8,128)(2,1)}) custom-call(bf16[64,16,64]{2,1,0:T(8,128)(2,1)} %align_ref.1, bf16[32,256,128]{2,1,0:T(8,128)(2,1)} %pair_hbm.1, bf16[32,64]{1,0:T(8,128)(2,1)} %bitcast.7, bf16[32,64]{1,0:T(8,128)(2,1)} %bitcast.8, ...), custom_call_target="tpu_custom_call" | custom-call | tf_op jit(solution)/shard_map/pallas_call | solution.py:532
  90.5 0.0 copy-start
  90.5 6.9 %shard_map.148 = (bf16[16,512,512]{2,1,0:T(8,128)(2,1)}, bf16[4,16,512]{2,1,0:T(8,128)(2,1)}) custom-call(bf16[16,512,128]{2,1,0:T(8,128)(2,1)} %get-tuple-element.11.turned_ref, bf16[128,512]{1,0:T(8,128)(2,1)} %proj_ref.3, bf16[4,128]{1,0:T(4,128)(2,1)} %bitcast.10), custom_call_target="tpu_custom_call" | custom-call | tf_op jit(solution)/shard_map/pallas_call | solution.py:590
  97.4 0.0 copy-done
  97.4 0.0 copy-start.1
  97.4 1.3 %copy.18 = bf16[32,256,128]{2,1,0:T(8,128)(2,1)} copy(bf16[32,256,128]{2,1,0:T(8,128)(2,1)S(1)} %copy-done) | data formatting | bytes 4194304
  98.8 0.0 copy-done.1
  98.8 0.7 copy.19
Async XLA Ops:
  90.5 6.9 %copy-start = (bf16[32,256,128]{2,1,0:T(8,128)(2,1)S(1)}, bf16[32,256,128]{2,1,0:T(8,128)(2,1)}, u32[]{:S(2)}) copy-start(bf16[32,256,128]{2,1,0:T(8,128)(2,1)} %get-tuple-element.18) | copy-start | bytes 6291460
  97.4 1.3 %copy-start.1 = (bf16[64,16,64]{2,1,0:T(8,128)(2,1)S(1)}, bf16[64,16,64]{2,1,0:T(8,128)(2,1)}, u32[]{:S(2)}) copy-start(bf16[64,16,64]{2,1,0:T(8,128)(2,1)} %get-tuple-element.19) | copy-start | bytes 393220
